TPU v7x, 32 devices: a whole 2x2x4 slice. The times are simulated.
32 devices in a mesh: groups: 2 (over y), req: 4 (over z), head: 4 (over x, core).
Axes of the slice: x: 2, y: 2, z: 4, core: 2. Of those that a mesh axis runs over, the one named last changes fastest.
Arguments:
- prompt_states: bfloat16 [4096, 8192], P(('groups', 'req'), 'head'), parts along dimension 0, may hold values from -6 to 6
- norm_gain: bfloat16 [8192], replicated, may hold values from 0.099609375 to 1.8984375
- key_weight: bfloat16 [8192, 1024], P('req', 'head'), may hold values from -0.0625 to 0.0625
- value_weight: bfloat16 [8192, 1024], P('req', 'head'), may hold values from -0.0625 to 0.0625
- block_owner: int32 [512, 1], P(('groups', 'req')), parts along dimension 0, may hold values from 0 to 3; in each aligned block of 64 rows (0 to 63, 64 to 127, ...) at most 22 rows name the same one
- block_slot: int32 [512], P(('groups', 'req')), parts along dimension 0, may hold values from 0 to 1
- block_len: int32 [512], P(('groups', 'req')), parts along dimension 0, may hold values from 1 to 8
- cache_key: bfloat16 [16, 1024, 1024], P(('groups', 'req'), None, 'head'), parts along dimension 0
- cache_value: bfloat16 [16, 1024, 1024], P(('groups', 'req'), None, 'head'), parts along dimension 0, may hold values from -6 to 6
- cache_len: int32 [16], P(('groups', 'req')), parts along dimension 0, may hold values from 2 to 1024
- query: bfloat16 [16, 2, 8192], P(('groups', 'req'), None, 'head'), parts along dimension 0
- step_key: bfloat16 [16, 2, 1024], P(('groups', 'req'), None, 'head'), parts along dimension 0, may hold values from -6 to 6
- step_value: bfloat16 [16, 2, 1024], P(('groups', 'req'), None, 'head'), parts along dimension 0, may hold values from -6 to 6
- out_weight: bfloat16 [8192, 8192], P('head', 'req'), may hold values from -0.0625 to 0.0625
Outputs:
- decoded: bfloat16 [16, 2, 8192], P(('groups', 'head'), None, 'req'), parts along dimension 0
There are 2 independent parts, one for each index of `groups`. A program takes and returns all parts, laid end to end along the dimension named above; an argument that names none is the same for every part. Nothing has to cross between parts.
Inputs may be any that keep to these rules, and one draw needn't show every extreme that they name: `block_owner`: among the 64 blocks of one index of req no decode index is named more than 22 times, a bound that some block reaches.
All inputs are finite; a program needn't handle non-finite values.
Results may differ from a plain program's by a relative error of at most 0.0095.
Values may be sent and summed in bfloat16 or wider, within the bound.
A program may use at most 128 MiB of HBM per device.

v0:
```python
import jax
import jax.numpy as jnp
from jax import lax
from jax.sharding import PartitionSpec as P

QPK = 8
HD = 128
BLK = 8


NEGATIVE = -1e30


def merge_scores(state, scores, valid, values, form):
    top, total, accum = state
    masked = jnp.where(valid, scores, NEGATIVE)
    new_top = jnp.maximum(top, jnp.max(masked, axis=-1))
    weights = jnp.where(valid, jnp.exp(masked - new_top[..., None]), 0.0)
    factor = jnp.exp(top - new_top)
    total = total * factor + jnp.sum(weights, axis=-1)
    accum = accum * factor[..., None] + jnp.einsum(form, weights, values)
    return (new_top, total, accum)


def attend_blocks(state, queries, kv_piece, slot, length, scale):
    count = kv_piece.shape[0]
    heads = queries.shape[2]
    width = kv_piece.shape[2] // 2
    keys = kv_piece[:, :, :width].reshape(count * BLK, heads, HD)
    values = kv_piece[:, :, width:].reshape(count * BLK, heads, HD).astype(jnp.float32)
    scores = (
        jnp.einsum("rshgd,thd->rshgt", queries, keys, preferred_element_type=jnp.float32) * scale
    )
    requests = queries.shape[0]
    token_ok = jnp.arange(BLK, dtype=jnp.int32)[None, :] < length[:, None]
    mine = slot[None, :] == jnp.arange(requests, dtype=jnp.int32)[:, None]
    valid = (mine[:, :, None] & token_ok[None, :, :]).reshape(requests, 1, 1, 1, count * BLK)
    return merge_scores(state, scores, valid, values, "rshgt,thd->rshgd")


def body(
    prompt_states,
    norm_gain,
    key_weight,
    value_weight,
    block_owner,
    block_slot,
    block_len,
    cache_key,
    cache_value,
    cache_len,
    query,
    step_key,
    step_value,
    out_weight,
):
    heads = query.shape[2] // (QPK * HD)
    width = heads * HD
    tokens = prompt_states.shape[0]
    whole = lax.all_gather(prompt_states, "head", axis=1, tiled=True)
    states = whole.astype(jnp.float32)
    stat = jnp.mean(states * states, axis=-1, keepdims=True)
    scaled = (states * norm_gain.astype(jnp.float32)).astype(jnp.bfloat16)
    factor = lax.rsqrt(stat + 1e-05)
    key_sum = jnp.dot(
        scaled,
        lax.all_gather(key_weight, "req", axis=0, tiled=True),
        preferred_element_type=jnp.float32,
    )
    value_sum = jnp.dot(
        scaled,
        lax.all_gather(value_weight, "req", axis=0, tiled=True),
        preferred_element_type=jnp.float32,
    )
    kv_rows = jnp.concatenate(
        [(key_sum * factor).astype(jnp.bfloat16), (value_sum * factor).astype(jnp.bfloat16)], axis=1
    )
    blocks_dev = tokens // BLK
    kv_blocks = kv_rows.reshape(blocks_dev, BLK, 2 * width)
    requests = query.shape[0]
    steps = query.shape[1]
    scale = 1.0 / HD**0.5
    queries = query.reshape(requests, steps, heads, QPK, HD)
    slots = cache_key.shape[1]
    cache_keys = cache_key.reshape(requests, slots, heads, HD)
    cache_values = cache_value.reshape(requests, slots, heads, HD).astype(jnp.float32)
    top = jnp.full((requests, steps, heads, QPK), NEGATIVE, jnp.float32)
    state = (top, jnp.zeros_like(top), jnp.zeros((requests, steps, heads, QPK, HD), jnp.float32))
    scores = (
        jnp.einsum("rshgd,rthd->rshgt", queries, cache_keys, preferred_element_type=jnp.float32)
        * scale
    )
    valid = (jnp.arange(slots, dtype=jnp.int32)[None, :] < cache_len[:, None])[
        :, None, None, None, :
    ]
    state = merge_scores(state, scores, valid, cache_values, "rshgt,rthd->rshgd")
    own_keys = step_key.reshape(requests, steps, heads, HD)
    own_values = step_value.reshape(requests, steps, heads, HD).astype(jnp.float32)
    scores = (
        jnp.einsum("rshgd,rphd->rshgp", queries, own_keys, preferred_element_type=jnp.float32)
        * scale
    )
    earlier = (jnp.arange(steps)[None, :] <= jnp.arange(steps)[:, None])[None, :, None, None, :]
    state = merge_scores(state, scores, earlier, own_values, "rshgp,rphd->rshgd")
    width_req = lax.axis_size("req")
    capacity = max(2, (4 * blocks_dev + 3 * width_req - 1) // (3 * width_req))
    target = block_owner[:, 0]
    onehot = (target[:, None] == jnp.arange(width_req, dtype=jnp.int32)[None, :]).astype(jnp.int32)
    before = jnp.cumsum(onehot, axis=0) - onehot
    rank = jnp.sum(before * onehot, axis=1)
    place = target * capacity + rank
    select = jnp.arange(width_req * capacity, dtype=jnp.int32)[:, None] == place[None, :]
    packed = jnp.dot(
        select.astype(jnp.bfloat16),
        kv_blocks.reshape(blocks_dev, BLK * 2 * width),
        preferred_element_type=jnp.float32,
    )
    packed = packed.astype(jnp.bfloat16).reshape(width_req, capacity, BLK, 2 * width)
    slot_sent = jnp.sum(jnp.where(select, block_slot[None, :], 0), axis=1)
    len_sent = jnp.sum(jnp.where(select, block_len[None, :], 0), axis=1)
    labels = jnp.stack([slot_sent, len_sent], axis=-1).reshape(width_req, capacity, 2)
    arrived, arrived_labels = (
        lax.all_to_all(packed, "req", split_axis=0, concat_axis=0, tiled=True),
        lax.all_to_all(labels, "req", split_axis=0, concat_axis=0, tiled=True),
    )
    arrived_labels = arrived_labels.reshape(width_req * capacity, 2)
    state = attend_blocks(
        state,
        queries,
        arrived.reshape(width_req * capacity, BLK, 2 * width),
        arrived_labels[:, 0],
        arrived_labels[:, 1],
        scale,
    )
    top, total, accum = state
    attention = (
        (accum / total[..., None]).reshape(requests, steps, heads * QPK * HD).astype(jnp.bfloat16)
    )
    piece = lax.all_gather(attention, "req", axis=0, tiled=True)
    count = piece.shape[0]
    product = jnp.dot(
        piece.reshape(count * steps, heads * QPK * HD),
        out_weight,
        preferred_element_type=jnp.float32,
    )
    terms = product.reshape(count, steps, out_weight.shape[1])
    return lax.psum_scatter(terms, "head", scatter_dimension=0, tiled=True).astype(jnp.bfloat16)


def solution(mesh):
    placed = (
        P(("groups", "req"), "head"),
        P(),
        P("req", "head"),
        P("req", "head"),
        P(("groups", "req"), None),
        P(("groups", "req")),
        P(("groups", "req")),
        P(("groups", "req"), None, "head"),
        P(("groups", "req"), None, "head"),
        P(("groups", "req")),
        P(("groups", "req"), None, "head"),
        P(("groups", "req"), None, "head"),
        P(("groups", "req"), None, "head"),
        P("head", "req"),
    )
    return jax.shard_map(
        body,
        mesh=mesh,
        in_specs=placed,
        out_specs=P(("groups", "head"), None, "req"),
        check_vma=False,
    )
```

profile of v0, /device:TPU:0, one launch (start us, length us, event | category | flops | bytes accessed | tf_op | source)
XLA Modules:
  0.0 303.0 jit_solution(12350330222061504837)
XLA Ops:
  6.5 0.7 all-gather.4.cloned.1.call-update
  7.3 0.7 all-gather.8.cloned.1.call-update
  8.1 0.7 all-gather.6.cloned.1.call-update
  8.7 0.7 fusion.43
  9.5 0.1 reduce_window_sum.11
  9.6 0.8 select_reduce_fusion.2
  10.4 0.7 multiply_add_fusion
  11.1 0.8 select_reduce_fusion.1
  11.9 0.1 stack.10
  12.0 0.6 copy.108
  12.6 6.3 %all-to-all-start = ((s32[4,22,2]{1,2,0:T(2,128)}), s32[4,22,2]{1,2,0:T(2,128)S(1)}, u32[]{:S(2)}, u32[]{:S(2)}) async-start(s32[4,22,2]{1,2,0:T(2,128)} %copy.108), calls=%async_computation | async-start | bytes 8192 | tf_op jit(solution)/shard_map/all_to_all | solution.py:124
  19.0 0.7 convert_element_type.36
  19.7 0.7 reshape.196
  20.4 0.1 lt.42
  20.5 1.6 reshape.195
  22.1 1.7 reshape.197
  23.8 0.6 dynamic-slice
  24.9 0.2 fusion.58
  25.2 44.8 %all-gather.4.cloned.1.call-done = bf16[512,8192]{1,0:T(8,128)(2,1)} async-done(((bf16[512,2048]{1,0:T(8,128)(2,1)}), bf16[512,8192]{1,0:T(8,128)(2,1)}) %all-gather.4.cloned.1.call-update) | async-done | bytes 8388624 | tf_op jit(solution)/shard_map/all_gather | solution.py:60
  69.9 5.1 %fusion.1 = f32[512]{0:T(512)S(1)} fusion(bf16[512,8192]{1,0:T(8,128)(2,1)} %all-gather.4.cloned.1.call-done), kind=kLoop, calls=%fused_computation.3 | loop fusion | flops 12582400 | bytes 8390656 | tf_op jit(solution)/shard_map/reduce_sum | solution.py:62
  75.1 77.3 %all-gather.8.cloned.1.call-done = bf16[8192,256]{1,0:T(8,128)(2,1)} async-done(((bf16[2048,256]{1,0:T(8,128)(2,1)}), bf16[8192,256]{1,0:T(8,128)(2,1)}) %all-gather.8.cloned.1.call-update) | async-done | bytes 4194320 | tf_op jit(solution)/shard_map/all_gather | solution.py:72
  152.3 7.0 %fusion.14 = bf16[512,256]{0,1:T(8,128)(2,1)S(1)} fusion(bf16[8192,256]{1,0:T(8,128)(2,1)} %all-gather.8.cloned.1.call-done, bf16[512,8192]{1,0:T(8,128)(2,1)} %all-gather.4.cloned.1.call-done, f32[8192]{0:T(1024)S(1)} %convert_element_type.36, f32[512]{0:T(512)S(1)} %add_rsqrt_fusion), kind=kOutput, calls=%fused_computation.11 | convolution fusion | flops 2160328704 | bytes 12879872 | tf_op jit(solution)/shard_map/dot_general | solution.py:70
  159.3 73.9 %all-gather.6.cloned.1.call-done = bf16[8192,256]{1,0:T(8,128)(2,1)} async-done(((bf16[2048,256]{1,0:T(8,128)(2,1)}), bf16[8192,256]{1,0:T(8,128)(2,1)}) %all-gather.6.cloned.1.call-update) | async-done | bytes 4194320 | tf_op jit(solution)/shard_map/all_gather | solution.py:67
  233.2 7.0 %fusion.17 = bf16[512,256]{0,1:T(8,128)(2,1)S(1)} fusion(bf16[8192,256]{1,0:T(8,128)(2,1)} %all-gather.6.cloned.1.call-done, bf16[512,8192]{1,0:T(8,128)(2,1)} %all-gather.4.cloned.1.call-done, f32[8192]{0:T(1024)S(1)} %convert_element_type.36, f32[512]{0:T(512)S(1)} %add_rsqrt_fusion), kind=kOutput, calls=%fused_computation.12 | convolution fusion | flops 2160328704 | bytes 12879872 | tf_op jit(solution)/shard_map/dot_general | solution.py:65
  240.2 0.2 copy.110
  240.4 0.2 reshape_reshape.3
  240.7 0.5 convolution_convert_fusion
  241.1 1.1 copy.137
  242.3 3.5 %all-to-all-start.1 = ((bf16[4,22,8,512]{3,2,1,0:T(8,128)(2,1)}), bf16[4,22,8,512]{3,2,1,0:T(8,128)(2,1)S(1)}, u32[]{:S(2)}, u32[]{:S(2)}) async-start(bf16[4,22,8,512]{3,2,1,0:T(8,128)(2,1)} %bitcast.30), calls=%async_computation.1 | async-start | bytes 1441792 | tf_op jit(solution)/shard_map/all_to_all | solution.py:123
  245.8 0.5 fusion.59
  246.3 0.1 reshape.200
  246.4 0.1 and.19
  246.5 0.1 and.20
  246.7 0.1 lt.44
  246.8 17.9 %all-to-all-done.1 = bf16[4,22,8,512]{3,2,1,0:T(8,128)(2,1)S(1)} async-done(((bf16[4,22,8,512]{3,2,1,0:T(8,128)(2,1)}), bf16[4,22,8,512]{3,2,1,0:T(8,128)(2,1)S(1)}, u32[]{:S(2)}, u32[]{:S(2)}) %all-to-all-start.1) | async-done | bytes 720928 | tf_op jit(solution)/shard_map/all_to_all | solution.py:123
  264.8 0.1 reshape.204
  264.9 0.1 reshape.203
  264.9 0.3 fusion.57
  265.3 0.2 fusion.54
  265.5 0.2 convolution_bitcast_fusion.2
  265.7 0.1 fusion.50
  265.8 0.2 fusion.37
  266.0 0.3 fusion.29
  266.4 0.3 fusion.30
  266.7 13.1 %all_gather.15 = bf16[8,2,2048]{2,1,0:T(2,128)(2,1)S(1)} all-gather(bf16[2,2,2048]{2,1,0:T(2,128)(2,1)S(1)} %convert_element_type.42), channel_id=1, replica_groups=mesh['groups'=2,'req'=4,'head'=4] {'req'}, dimensions={0}, use_global_device_ids=true | all-gather | bytes 81920 | tf_op jit(solution)/shard_map/all_gather | solution.py:139
  279.8 4.6 %fusion.2 = f32[8,2,2048]{2,0,1:T(8,128)S(1)} fusion(bf16[2048,2048]{1,0:T(8,128)(2,1)} %param.27, bf16[8,2,2048]{2,1,0:T(2,128)(2,1)S(1)} %all_gather.15), kind=kOutput, calls=%fused_computation.4 | convolution fusion | flops 134217728 | bytes 8585216 | tf_op jit(solution)/shard_map/dot_general | solution.py:141
  284.4 11.5 %all-reduce.2 = bf16[8,2,2048]{2,0,1:T(8,128)(2,1)S(1)} all-reduce(f32[8,2,2048]{2,0,1:T(8,128)S(1)} %fusion.2), channel_id=2, replica_groups=mesh['groups'=2,'req'=4,'head'=4] {'head'}, use_global_device_ids=true, to_apply=%region_11.12.clone | all-reduce | flops 32768 | bytes 196608
  295.9 0.6 copy.120
  (31 shorter events, 0.6 us)
Async XLA Ops:
  6.5 259.8 %copy-start = (bf16[2,2,256]{2,1,0:T(2,128)(2,1)S(1)}, bf16[2,2,256]{2,1,0:T(2,128)(2,1)}, u32[]{:S(2)}) copy-start(bf16[2,2,256]{2,1,0:T(2,128)(2,1)} %param.26) | copy-start | bytes 6148
  6.5 17.2 %copy-start.3 = (u32[32]{0:T(128)S(1)}, u32[32]{0:T(128)}, u32[]{:S(2)}) copy-start(u32[32]{0:T(128)} %constant.34) | copy-start | bytes 388
  6.5 18.4 %copy-start.2 = (bf16[2,2,256]{2,1,0:T(2,128)(2,1)S(1)}, bf16[2,2,256]{2,1,0:T(2,128)(2,1)}, u32[]{:S(2)}) copy-start(bf16[2,2,256]{2,1,0:T(2,128)(2,1)} %param.25) | copy-start | bytes 6148
  6.5 63.4 %all-gather.4.cloned.1.call-start = ((), (), s32[]{:S(2)}) async-start(), calls=%async_computation.2 | async-start | bytes 10485760 | tf_op jit(solution)/shard_map/all_gather | solution.py:60
  7.3 145.0 %all-gather.8.cloned.1.call-start = ((), (), s32[]{:S(2)}) async-start(), calls=%async_computation.4 | async-start | bytes 5242880 | tf_op jit(solution)/shard_map/all_gather | solution.py:72
  8.0 225.2 %all-gather.6.cloned.1.call-start = ((), (), s32[]{:S(2)}) async-start(), calls=%async_computation.3 | async-start | bytes 5242880 | tf_op jit(solution)/shard_map/all_gather | solution.py:67
  12.6 229.6 %all-to-all-start = ((s32[4,22,2]{1,2,0:T(2,128)}), s32[4,22,2]{1,2,0:T(2,128)S(1)}, u32[]{:S(2)}, u32[]{:S(2)}) async-start(s32[4,22,2]{1,2,0:T(2,128)} %copy.108), calls=%async_computation | async-start | bytes 8192 | tf_op jit(solution)/shard_map/all_to_all | solution.py:124
  159.3 86.5 %copy-start.1 = (s32[2]{0:T(128)S(1)}, s32[2]{0:T(128)}, u32[]{:S(2)}) copy-start(s32[2]{0:T(128)} %param.23) | copy-start | bytes 28
  242.3 22.5 %all-to-all-start.1 = ((bf16[4,22,8,512]{3,2,1,0:T(8,128)(2,1)}), bf16[4,22,8,512]{3,2,1,0:T(8,128)(2,1)S(1)}, u32[]{:S(2)}, u32[]{:S(2)}) async-start(bf16[4,22,8,512]{3,2,1,0:T(8,128)(2,1)} %bitcast.30), calls=%async_computation.1 | async-start | bytes 1441792 | tf_op jit(solution)/shard_map/all_to_all | solution.py:123
Sparse Core Ops, SparseCore 0:
  8.9 60.9 all-gather.3
  71.5 80.7 all-gather.7
  153.9 79.2 all-gather.5
where the time goes:
time: 304 us; the launch traced here: 303 us
  waiting for transfers between devices  216 us (71%)
  blocking collectives  24.6 us (8%)
  matrix products  20.7 us (7%)
  between operations  13.9 us (5%)
  starting transfers between devices  9.88 us (3%)
  other arithmetic  9.63 us (3%)
  local copies, waits for them, and re-layouts  8.34 us (3%)
    all_gather x1, waiting for transfers between devices, body(): lax.all_gather(value_weight, 'req', axis=0, tiled=True)  77.3 us
    all_gather x1, waiting for transfers between devices, body(): lax.all_gather(key_weight, 'req', axis=0, tiled=True)  73.9 us
    all_gather x1, waiting for transfers between devices, body(): whole = lax.all_gather(prompt_states, 'head', axis=1, tiled=True)  44.8 us
    all_to_all x1, waiting for transfers between devices, body(): lax.all_to_all(packed, 'req', split_axis=0, concat_axis=0, tiled=True)  17.9 us
    all_gather x1, blocking collectives, body(): piece = lax.all_gather(attention, 'req', axis=0, tiled=True)  13.1 us
    unnamed x1, blocking collectives  11.5 us
    dot_general x1, matrix products, body(): jnp.dot(scaled, lax.all_gather(value_weight, 'req', axis=0, tiled=True),...  6.96 us
    dot_general x1, matrix products, body(): jnp.dot(scaled, lax.all_gather(key_weight, 'req', axis=0, tiled=True), pr...  6.95 us
  transfers between devices with their start and end apart: 5, of which 4 were waited for; matrix products, arithmetic and copies ran while one was open for 10% of the time, Pallas kernels for 0%

commit v1 on v0

v1 whole, which is shorter than its diff:
```python
import functools

import jax
import jax.numpy as jnp
from jax import lax
from jax.experimental import pallas as pl
from jax.experimental.pallas import tpu as pltpu
from jax.sharding import PartitionSpec as P

QPK = 8
HD = 128
BLK = 8
NEGATIVE = -1e30
MESH = pl.DeviceIdType.MESH
F32 = jnp.float32
BF16 = jnp.bfloat16


def dot_t(a, b):
    return lax.dot_general(a, b, (((1,), (1,)), ((), ())), preferred_element_type=F32)


def kernel(
    nz, nh, pieces, xpieces,
    gain_ref, code_ref, clen_ref, q_ref, sk_ref, sv_ref,
    x_hbm, wk_hbm, wv_hbm, ck_hbm, cv_hbm, ow_hbm,
    out_ref,
    xraw, xbuf, wbuf, acc, ckv, owbuf, qbuf, psend, precv, cst, asend, arecv, af, osend, orecv, sbuf,
    loc, zs, zr, ys, yr, xs, xr, cs, cr, os_, or_, qs, qr, ps, pr, as_, ar, fs, fr, ss, sr,
):
    me_g = lax.axis_index("groups")
    me = lax.axis_index("req")
    mh = lax.axis_index("head")
    chip = mh // 2
    core = mh % 2
    nx = nh // 2
    sib = chip * 2 + (1 - core)
    tokens, xc = xraw.shape
    wr, width = wk_hbm.shape
    heads = width // HD
    wp = wr // pieces
    tp = tokens // xpieces
    reqs, steps = sk_ref.shape[0], sk_ref.shape[1]
    rq = steps * QPK
    own = reqs * rq
    scale = 1.0 / HD**0.5

    def at_z(p):
        return (me_g, p, mh)

    def at_h(h):
        return (me_g, me, h)

    peer_g = (1 - me_g, me, mh)

    def remote(src, dst, ssem, rsem, dev):
        return pltpu.make_async_remote_copy(
            src_ref=src, dst_ref=dst, send_sem=ssem, recv_sem=rsem, device_id=dev, device_id_type=MESH
        )

    cpx = pltpu.make_async_copy(x_hbm, xraw, loc.at[0])
    cpk = pltpu.make_async_copy(wk_hbm, wbuf.at[me, 0], loc.at[1])
    cpv = pltpu.make_async_copy(wv_hbm, wbuf.at[me, 1], loc.at[2])
    cck = pltpu.make_async_copy(ck_hbm, ckv.at[0], loc.at[3])
    ccv = pltpu.make_async_copy(cv_hbm, ckv.at[1], loc.at[4])
    cow = pltpu.make_async_copy(ow_hbm, owbuf, loc.at[5])
    for c in (cpk, cpv, cpx, cck, ccv, cow):
        c.start()

    barrier = pltpu.get_barrier_semaphore()
    for d in range(1, nz):
        pl.semaphore_signal(barrier, inc=1, device_id=at_z(lax.rem(me + d, nz)), device_id_type=MESH)
    for d in range(1, nh):
        pl.semaphore_signal(barrier, inc=1, device_id=at_h(lax.rem(mh + d, nh)), device_id_type=MESH)
    pl.semaphore_signal(barrier, inc=1, device_id=peer_g, device_id_type=MESH)
    pl.semaphore_wait(barrier, nz + nh - 1)

    pending = []

    def begin(cond, copy):
        pending.append((cond, copy))
        if cond is None:
            copy.start()
        else:
            pl.when(cond)(copy.start)

    def zcopy(d, i, chunk):
        dr = 1 - 2 * d
        k = i % pieces
        part = wbuf.at[chunk, me_g, pl.ds(k * wp, wp)]
        return remote(part, part, zs.at[d, i], zr.at[d, i], at_z(me + dr))

    def inside(v, n):
        return jnp.logical_and(v >= 0, v < n)

    cpk.wait()
    cpv.wait()
    for k in range(pieces):
        for d in range(2):
            begin(inside(me + 1 - 2 * d, nz), zcopy(d, k, me))

    for d in range(1, nz):
        begin(None, remote(q_ref, qbuf.at[me], qs.at[d - 1], qr.at[d - 1], at_z(lax.rem(me + d, nz))))
    qbuf[me] = q_ref[...]

    cpx.wait()

    def xcopy(d, e, c):
        dr = 1 - 2 * d
        k = e % xpieces
        part = xbuf.at[c, pl.ds(k * tp, tp)]
        return remote(part, part, xs.at[d, e], xr.at[d, e], at_h(mh + 2 * dr))

    ones = jnp.ones((8, xc), BF16)
    for k in range(xpieces):
        rows = pl.ds(k * tp, tp)
        xf = xraw[rows, :].astype(F32)
        xbuf[mh, rows, :] = (xf * gain_ref[...]).astype(BF16)
        for d in range(2):
            begin(inside(chip + 1 - 2 * d, nx), xcopy(d, k, mh))
        sq = xf * xf
        hi = sq.astype(BF16)
        lo = (sq - hi.astype(F32)).astype(BF16)
        sbuf[mh, :, k * tp : (k + 1) * tp] = dot_t(ones, hi) + dot_t(ones, lo)
    begin(None, remote(xbuf.at[mh], xbuf.at[mh], os_.at[0], or_.at[0], at_h(sib)))
    for d in range(1, nh):
        begin(None, remote(sbuf.at[mh], sbuf.at[mh], ss.at[d - 1], sr.at[d - 1], at_h(lax.rem(mh + d, nh))))

    cck.wait()
    ccv.wait()
    lane = lax.broadcasted_iota(jnp.int32, (1, 128), 1)
    slots = ckv.shape[2]
    for n in range(reqs):
        skf = sk_ref[n].astype(F32)
        svf = sv_ref[n].astype(F32)
        for g in range(heads):
            cols = slice(g * HD, (g + 1) * HD)
            q = q_ref[g, n * rq : (n + 1) * rq, :]
            s = dot_t(q, ckv[0, n, :, cols]) * scale
            ok = lax.broadcasted_iota(jnp.int32, (1, slots), 1) < clen_ref[n]
            s = jnp.where(ok, s, NEGATIVE)
            m = jnp.max(s, axis=-1, keepdims=True)
            qf = q.astype(F32)
            step = lax.broadcasted_iota(jnp.int32, (rq, 1), 0) // QPK
            own_s = []
            for p in range(steps):
                t = jnp.sum(qf * skf[p : p + 1, cols], axis=-1, keepdims=True) * scale
                t = jnp.where(step >= p, t, NEGATIVE)
                own_s.append(t)
                m = jnp.maximum(m, t)
            w = jnp.where(ok, jnp.exp(s - m), 0.0)
            total = jnp.sum(w, axis=-1, keepdims=True)
            a = jnp.dot(w.astype(BF16), ckv[1, n, :, cols], preferred_element_type=F32)
            for p in range(steps):
                u = jnp.where(step >= p, jnp.exp(own_s[p] - m), 0.0)
                total = total + u
                a = a + u * svf[p : p + 1, cols]
            cst[g, n * rq : (n + 1) * rq, 0:128] = a
            cst[g, n * rq : (n + 1) * rq, 128:256] = jnp.where(lane < 64, m, total)

    count = (nz - 1) * pieces
    xcount = (nx - 1) * xpieces

    def zrelay(i):
        for d in range(2):
            dr = 1 - 2 * d
            chunk = me - dr * (1 + i // pieces)
            good = inside(chunk, nz)
            pl.when(good)(zcopy(d, i, chunk).wait_recv)
            if i + pieces < count:
                begin(jnp.logical_and(good, inside(me + dr, nz)), zcopy(d, i + pieces, chunk))
            part = wbuf.at[chunk, me_g, pl.ds((i % pieces) * wp, wp)]
            begin(good, remote(part, part, ys.at[d, i], yr.at[d, i], peer_g))

    def xrelay(e):
        for d in range(2):
            dr = 1 - 2 * d
            c = chip - dr * (1 + e // xpieces)
            good = inside(c, nx)
            h = c * 2 + core
            pl.when(good)(xcopy(d, e, h).wait_recv)
            if e + xpieces < xcount:
                begin(jnp.logical_and(good, inside(chip + dr, nx)), xcopy(d, e + xpieces, h))
            part = xbuf.at[h, pl.ds((e % xpieces) * tp, tp)]
            begin(good, remote(part, part, cs.at[d, e], cr.at[d, e], at_h(sib)))

    def states_ready():
        remote(xbuf.at[sib], xbuf.at[sib], os_.at[0], or_.at[0], at_h(sib)).wait_recv()
        for e in range(xcount):
            for d in range(2):
                c = chip - (1 - 2 * d) * (1 + e // xpieces)
                part = xbuf.at[c * 2 + 1 - core, pl.ds((e % xpieces) * tp, tp)]
                pl.when(inside(c, nx))(remote(part, part, cs.at[d, e], cr.at[d, e], at_h(sib)).wait_recv)

    def multiply(chunk, k, fresh):
        at = chunk * wr + k * wp
        if wr == xc:
            lhs = xbuf[chunk, :, k * wp : (k + 1) * wp]
        else:
            lhs = xbuf[at // xc, :, pl.ds(pl.multiple_of(at % xc, 128), wp)]
        for j in range(2):
            prod = jnp.dot(lhs, wbuf[chunk, j, pl.ds(k * wp, wp), :], preferred_element_type=F32)
            acc[j] = prod if fresh else acc[j] + prod

    def consume(u):
        if u < pieces:
            multiply(me, u, u == 0)
            return
        i = u - pieces
        for d in range(2):
            chunk = me - (1 - 2 * d) * (1 + i // pieces)

            @pl.when(inside(chunk, nz))
            def _():
                part = wbuf.at[chunk, 1 - me_g, pl.ds((i % pieces) * wp, wp)]
                remote(part, part, ys.at[d, i], yr.at[d, i], peer_g).wait_recv()
                multiply(chunk, i % pieces, False)

    xdue = [max(0, (e + 1) * 2 * count // (3 * xcount) - 1) for e in range(xcount)]
    first = min(max(xdue) + 1, count - 1)
    done = 0
    for i in range(count):
        zrelay(i)
        for e in range(xcount):
            if xdue[e] == i:
                xrelay(e)
        if i == first:
            states_ready()
        if i >= first:
            goal = (pieces + i) * (i - first + 1) // (count - first)
            while done < goal:
                consume(done)
                done += 1
    while done < pieces + count:
        consume(done)
        done += 1

    for d in range(1, nz):
        src = qbuf.at[lax.rem(me - d + nz, nz)]
        remote(src, src, qs.at[d - 1], qr.at[d - 1], at_z(lax.rem(me + d, nz))).wait_recv()
    for d in range(1, nh):
        src = sbuf.at[lax.rem(mh - d + nh, nh)]
        remote(src, src, ss.at[d - 1], sr.at[d - 1], at_h(lax.rem(mh + d, nh))).wait_recv()
    stat = sbuf[0]
    for h in range(1, nh):
        stat = stat + sbuf[h]
    factor = lax.rsqrt(stat[0:1, :] * (1.0 / (nh * xc)) + 1e-05)
    rows = nz * own
    valid = code_ref[...] == lax.broadcasted_iota(jnp.int32, (rows, 1), 0) // rq
    for g in range(heads):
        cols = slice(g * HD, (g + 1) * HD)
        q = qbuf[:, g].reshape(rows, HD)
        s = dot_t(q, acc[0, :, cols].astype(BF16)) * (factor * scale)
        s = jnp.where(valid, s, NEGATIVE)
        m = jnp.max(s, axis=-1, keepdims=True)
        w = jnp.where(valid, jnp.exp(s - m), 0.0)
        total = jnp.sum(w, axis=-1, keepdims=True)
        a = jnp.dot((w * factor).astype(BF16), acc[1, :, cols].astype(BF16), preferred_element_type=F32)
        psend[:, g, :, 0:128] = a.reshape(nz, own, HD)
        psend[:, g, :, 128:256] = jnp.where(lane < 64, m, total).reshape(nz, own, 128)
    for d in range(1, nz):
        to = lax.rem(me + d, nz)
        begin(None, remote(psend.at[to], precv.at[me], ps.at[d - 1], pr.at[d - 1], at_z(to)))
    precv[me] = psend[me]
    for d in range(1, nz):
        src = precv.at[lax.rem(me - d + nz, nz)]
        remote(src, src, ps.at[d - 1], pr.at[d - 1], at_z(lax.rem(me + d, nz))).wait_recv()

    for g in range(heads):
        parts = [cst[g]] + [precv[p, g] for p in range(nz)]
        top = parts[0][:, 128:129]
        for t in parts[1:]:
            top = jnp.maximum(top, t[:, 128:129])
        total = jnp.zeros((own, 1), F32)
        a = jnp.zeros((own, HD), F32)
        for t in parts:
            e = jnp.exp(t[:, 128:129] - top)
            total = total + e * t[:, 192:193]
            a = a + e * t[:, 0:128]
        asend[g] = (a / total).astype(BF16)
    for d in range(1, nz):
        begin(None, remote(asend, arecv.at[me], as_.at[d - 1], ar.at[d - 1], at_z(lax.rem(me + d, nz))))
    arecv[me] = asend[...]
    for d in range(1, nz):
        src = arecv.at[lax.rem(me - d + nz, nz)]
        remote(src, src, as_.at[d - 1], ar.at[d - 1], at_z(lax.rem(me + d, nz))).wait_recv()

    cow.wait()
    for g in range(heads):
        af[g * nz * own : (g + 1) * nz * own, :] = arecv[:, g].reshape(nz * own, HD).astype(F32)
    every = nz * reqs * steps
    pieces_in = [
        af[pl.ds(g * nz * own + j, every, stride=QPK), :] for g in range(heads) for j in range(QPK)
    ]
    lhs = jnp.concatenate(pieces_in, axis=1).astype(BF16)
    prod = jnp.dot(lhs, owbuf[...], preferred_element_type=F32)
    ro = every // nh
    for h in range(nh):
        osend[h] = prod[h * ro : (h + 1) * ro, :]
    for d in range(1, nh):
        to = lax.rem(mh + d, nh)
        begin(None, remote(osend.at[to], orecv.at[mh], fs.at[d - 1], fr.at[d - 1], at_h(to)))
    orecv[mh] = osend[mh]
    for d in range(1, nh):
        src = orecv.at[lax.rem(mh - d + nh, nh)]
        remote(src, src, fs.at[d - 1], fr.at[d - 1], at_h(lax.rem(mh + d, nh))).wait_recv()
    final = orecv[0]
    for h in range(1, nh):
        final = final + orecv[h]
    final = final.astype(BF16)
    for n in range(ro // steps):
        out_ref[n] = final[n * steps : (n + 1) * steps, :]

    for cond, copy in pending:
        if cond is None:
            copy.wait_send()
        else:
            pl.when(cond)(copy.wait_send)


def body(
    prompt_states, norm_gain, key_weight, value_weight, block_owner, block_slot, block_len,
    cache_key, cache_value, cache_len, query, step_key, step_value, out_weight,
):
    nz, nh = lax.axis_size("req"), lax.axis_size("head")
    tokens, xc = prompt_states.shape
    wr, width = key_weight.shape
    heads = width // HD
    reqs, steps = query.shape[0], query.shape[1]
    own = reqs * steps * QPK
    oc = out_weight.shape[1]
    slots = cache_key.shape[1]
    gain = lax.dynamic_slice(norm_gain, (lax.axis_index("head") * xc,), (xc,)).astype(F32).reshape(1, xc)
    target = block_owner[:, 0] * reqs + block_slot
    code = jnp.where(jnp.arange(BLK, dtype=jnp.int32)[None, :] < block_len[:, None], target[:, None], -1)
    code = code.reshape(1, tokens)
    q = query.reshape(reqs, steps, heads, QPK, HD).transpose(2, 0, 1, 3, 4).reshape(heads, own, HD)
    pieces = max(1, wr // 512)
    xpieces = 4
    ro = nz * reqs // nh
    zc = (nz - 1) * pieces
    xcnt = (nh // 2 - 1) * xpieces
    dma = pltpu.SemaphoreType.DMA
    vm = pl.BlockSpec(memory_space=pltpu.VMEM)
    sm = pl.BlockSpec(memory_space=pltpu.SMEM)
    hb = pl.BlockSpec(memory_space=pl.ANY)
    return pl.pallas_call(
        functools.partial(kernel, nz, nh, pieces, xpieces),
        out_shape=jax.ShapeDtypeStruct((ro, steps, oc), BF16),
        in_specs=[vm, vm, sm, vm, vm, vm, hb, hb, hb, hb, hb, hb],
        out_specs=vm,
        scratch_shapes=[
            pltpu.VMEM((tokens, xc), BF16),
            pltpu.VMEM((nh, tokens, xc), BF16),
            pltpu.VMEM((nz, 2, wr, width), BF16),
            pltpu.VMEM((2, tokens, width), F32),
            pltpu.VMEM((2, reqs, slots, width), BF16),
            pltpu.VMEM(out_weight.shape, BF16),
            pltpu.VMEM((nz, heads, own, HD), BF16),
            pltpu.VMEM((nz, heads, own, 256), F32),
            pltpu.VMEM((nz, heads, own, 256), F32),
            pltpu.VMEM((heads, own, 256), F32),
            pltpu.VMEM((heads, own, HD), BF16),
            pltpu.VMEM((nz, heads, own, HD), BF16),
            pltpu.VMEM((heads * nz * own, HD), F32),
            pltpu.VMEM((nh, ro * steps, oc), F32),
            pltpu.VMEM((nh, ro * steps, oc), F32),
            pltpu.VMEM((nh, 8, tokens), F32),
            dma((6,)),
            dma((2, zc)), dma((2, zc)), dma((2, zc)), dma((2, zc)),
            dma((2, xcnt)), dma((2, xcnt)), dma((2, xcnt)), dma((2, xcnt)),
            dma((1,)), dma((1,)),
            dma((nz - 1,)), dma((nz - 1,)), dma((nz - 1,)), dma((nz - 1,)), dma((nz - 1,)), dma((nz - 1,)),
            dma((nh - 1,)), dma((nh - 1,)), dma((nh - 1,)), dma((nh - 1,)),
        ],
        compiler_params=pltpu.CompilerParams(
            collective_id=0, has_side_effects=True, vmem_limit_bytes=52 * 1024 * 1024
        ),
    )(
        gain, code, cache_len, q, step_key, step_value,
        prompt_states, key_weight, value_weight, cache_key, cache_value, out_weight,
    )


def solution(mesh):
    placed = (
        P(("groups", "req"), "head"),
        P(),
        P("req", "head"),
        P("req", "head"),
        P(("groups", "req"), None),
        P(("groups", "req")),
        P(("groups", "req")),
        P(("groups", "req"), None, "head"),
        P(("groups", "req"), None, "head"),
        P(("groups", "req")),
        P(("groups", "req"), None, "head"),
        P(("groups", "req"), None, "head"),
        P(("groups", "req"), None, "head"),
        P("head", "req"),
    )
    return jax.shard_map(
        body,
        mesh=mesh,
        in_specs=placed,
        out_specs=P(("groups", "head"), None, "req"),
        check_vma=False,
    )
```

time: 304 us -> 107 us (0.35)
  waiting for transfers between devices: 216 us -> 0 us
  Pallas kernels: 0 us -> 100 us
  blocking collectives: 24.6 us -> 0 us
  matrix products: 20.7 us -> 0 us
  between operations: 13.9 us -> 0.04 us
  starting transfers between devices: 9.88 us -> 0 us
  other arithmetic: 9.63 us -> 2.09 us
  local copies, waits for them, and re-layouts: 8.34 us -> 4.68 us
    all_gather x3 -> x0, waiting for transfers between devices: 196 us -> none  [the longest x1 77.3 us: body(): lax.all_gather(value_weight, 'req', axis=0, tiled=True)]
    pallas_call x0 -> x1, Pallas kernels: none -> 100 us  [body(): pl.pallas_call(functools.partial(kernel, nz, nh, pieces, xpieces), out_sh...]
    dot_general x10 -> x0, matrix products: 20.7 us -> none  [the longest x1 6.96 us: body(): jnp.dot(scaled, lax.all_gather(value_weight, 'req', axis=0, tiled=True),...]
    all_to_all x2 -> x0, waiting for transfers between devices: 17.9 us -> none  [the longest x1 17.9 us: body(): lax.all_to_all(packed, 'req', split_axis=0, concat_axis=0, tiled=True)]
    all_gather x1 -> x0, blocking collectives: 13.1 us -> none  [body(): piece = lax.all_gather(attention, 'req', axis=0, tiled=True)]
    unnamed x1 -> x0, blocking collectives: 11.5 us -> none
    all_to_all x2 -> x0, starting transfers between devices: 9.81 us -> none  [the longest x1 6.32 us: body(): lax.all_to_all(labels, 'req', split_axis=0, concat_axis=0, tiled=True)]
    reduce_sum x6 -> x0, other arithmetic: 7.21 us -> none  [the longest x1 5.1 us: body(): stat = jnp.mean(states * states, axis=-1, keepdims=True)]
  transfers between devices with their start and end apart: 5 -> 0, of which waited for: 4 -> 0; matrix products, arithmetic and copies ran while one was open for 10% -> 0% of each run, Pallas kernels for 0% -> 0%
where the time goes in v1:
time: 107 us
  Pallas kernels  100 us (93%)
  local copies, waits for them, and re-layouts  4.68 us (4%)
  other arithmetic  2.09 us (2%)
    pallas_call x1, Pallas kernels, body(): pl.pallas_call(functools.partial(kernel, nz, nh, pieces, xpieces), out_sh...  100 us
    unnamed x9, local copies, waits for them, and re-layouts  3.84 us

profile of v1, /device:TPU:0, one launch (start us, length us, event | category | flops | bytes accessed | tf_op | source)
XLA Modules:
  0.0 106.9 jit_solution(4659004238126271358)
XLA Ops:
  0.0 0.7 dynamic-slice_convert_fusion
  0.7 0.7 bitcast_add_fusion
  1.4 0.7 fusion
  2.1 0.1 select_n.19.code_ref
  2.2 0.7 reshape.54
  2.9 0.0 copy-start
  3.0 1.2 %copy-done = bf16[2048,256]{1,0:T(8,128)(2,1)S(1)} copy-done((bf16[2048,256]{1,0:T(8,128)(2,1)S(1)}, bf16[2048,256]{1,0:T(8,128)(2,1)}, u32[]{:S(2)}) %copy-start) | copy-done | bytes 1048600
  4.2 0.0 copy-start.1
  4.2 0.7 copy-done.1
  4.9 0.0 copy-start.2
  4.9 0.7 copy-done.2
  5.5 0.0 copy-start.3
  5.5 0.7 copy-done.3
  6.2 100.1 %shard_map.136 = bf16[2,2,2048]{2,1,0:T(2,128)(2,1)S(1)} custom-call(f32[1,2048]{1,0:T(1,128)S(1)} %bitcast.7, s32[1,512]{1,0:T(1,128)S(1)} %select_n.19.code_ref, s32[2]{0:T(128)S(1)} %copy-done.3, bf16[2,32,128]{2,1,0:T(8,128)(2,1)S(1)} %bitcast.6, bf16[2,2,256]{2,1,0:T(2,128)(2,1)S(1)} %copy-done.1, bf16[2,2,256]{2,1,0:T(2,128)(2,1)S(1)} %copy-done.2, ...), custom_call_target="tpu_custom_call" | custom-call | tf_op jit(solution)/shard_map/pallas_call | solution.py:347
  106.3 0.6 copy.18
  (1 shorter events, 0.0 us)
Async XLA Ops:
  2.9 1.2 %copy-start = (bf16[2048,256]{1,0:T(8,128)(2,1)S(1)}, bf16[2048,256]{1,0:T(8,128)(2,1)}, u32[]{:S(2)}) copy-start(bf16[2048,256]{1,0:T(8,128)(2,1)} %wk_hbm.1) | copy-start | bytes 3145732
  4.2 0.7 copy-start.1
  4.9 0.7 copy-start.2
  5.5 0.7 copy-start.3

commit v2 on v1

--- a/solution.py
+++ b/solution.py
@@ -22,9 +22,10 @@
 
 def kernel(
     nz, nh, pieces, xpieces,
-    gain_ref, code_ref, clen_ref, q_ref, sk_ref, sv_ref,
+    gain_hbm, owner_hbm, slot_hbm, len_hbm, clen_hbm, query_hbm, sk_hbm, sv_hbm,
     x_hbm, wk_hbm, wv_hbm, ck_hbm, cv_hbm, ow_hbm,
     out_ref,
+    gain_ref, owner_ref, slot_ref, len_ref, clen_ref, query_ref, sk_ref, sv_ref, qf_ref, q_ref,
     xraw, xbuf, wbuf, acc, ckv, owbuf, qbuf, psend, precv, cst, asend, arecv, af, osend, orecv, sbuf,
     loc, zs, zr, ys, yr, xs, xr, cs, cr, os_, or_, qs, qr, ps, pr, as_, ar, fs, fr, ss, sr,
 ):
@@ -64,7 +65,16 @@
     cck = pltpu.make_async_copy(ck_hbm, ckv.at[0], loc.at[3])
     ccv = pltpu.make_async_copy(cv_hbm, ckv.at[1], loc.at[4])
     cow = pltpu.make_async_copy(ow_hbm, owbuf, loc.at[5])
-    for c in (cpk, cpv, cpx, cck, ccv, cow):
+    small = [
+        pltpu.make_async_copy(src, dst, loc.at[6 + i])
+        for i, (src, dst) in enumerate(
+            [
+                (query_hbm, query_ref), (gain_hbm, gain_ref), (owner_hbm, owner_ref), (slot_hbm, slot_ref),
+                (len_hbm, len_ref), (clen_hbm, clen_ref), (sk_hbm, sk_ref), (sv_hbm, sv_ref),
+            ]
+        )
+    ]
+    for c in (cpk, cpv, cpx, *small, cck, ccv, cow):
         c.start()
 
     barrier = pltpu.get_barrier_semaphore()
@@ -99,11 +109,21 @@
         for d in range(2):
             begin(inside(me + 1 - 2 * d, nz), zcopy(d, k, me))
 
+    small[0].wait()
+    for n in range(reqs):
+        both = query_ref[n].astype(F32)
+        for g in range(heads):
+            for j in range(QPK):
+                lanes = (g * QPK + j) * HD
+                qf_ref[pl.ds(g * own + n * rq + j, steps, stride=QPK), :] = both[:, lanes : lanes + HD]
+    q_ref[...] = qf_ref[...].astype(BF16).reshape(heads, own, HD)
     for d in range(1, nz):
         begin(None, remote(q_ref, qbuf.at[me], qs.at[d - 1], qr.at[d - 1], at_z(lax.rem(me + d, nz))))
     qbuf[me] = q_ref[...]
 
     cpx.wait()
+    small[1].wait()
+    gain = gain_ref[pl.ds(pl.multiple_of(mh * xc, 128), xc)].astype(F32).reshape(1, xc)
 
     def xcopy(d, e, c):
         dr = 1 - 2 * d
@@ -115,7 +135,7 @@
     for k in range(xpieces):
         rows = pl.ds(k * tp, tp)
         xf = xraw[rows, :].astype(F32)
-        xbuf[mh, rows, :] = (xf * gain_ref[...]).astype(BF16)
+        xbuf[mh, rows, :] = (xf * gain).astype(BF16)
         for d in range(2):
             begin(inside(chip + 1 - 2 * d, nx), xcopy(d, k, mh))
         sq = xf * xf
@@ -126,6 +146,15 @@
     for d in range(1, nh):
         begin(None, remote(sbuf.at[mh], sbuf.at[mh], ss.at[d - 1], sr.at[d - 1], at_h(lax.rem(mh + d, nh))))
 
+    for c in small[2:]:
+        c.wait()
+    token = lax.broadcasted_iota(jnp.int32, (1, tokens), 1)
+
+    def name_block(b, code):
+        named = jnp.where(token % BLK < len_ref[b], owner_ref[b] * reqs + slot_ref[b], -1)
+        return jnp.where(token // BLK == b, named, code)
+
+    code = lax.fori_loop(0, tokens // BLK, name_block, jnp.full((1, tokens), -1, jnp.int32))
     cck.wait()
     ccv.wait()
     lane = lax.broadcasted_iota(jnp.int32, (1, 128), 1)
@@ -246,7 +275,7 @@
         stat = stat + sbuf[h]
     factor = lax.rsqrt(stat[0:1, :] * (1.0 / (nh * xc)) + 1e-05)
     rows = nz * own
-    valid = code_ref[...] == lax.broadcasted_iota(jnp.int32, (rows, 1), 0) // rq
+    valid = code == lax.broadcasted_iota(jnp.int32, (rows, 1), 0) // rq
     for g in range(heads):
         cols = slice(g * HD, (g + 1) * HD)
         q = qbuf[:, g].reshape(rows, HD)
@@ -256,8 +285,16 @@
         w = jnp.where(valid, jnp.exp(s - m), 0.0)
         total = jnp.sum(w, axis=-1, keepdims=True)
         a = jnp.dot((w * factor).astype(BF16), acc[1, :, cols].astype(BF16), preferred_element_type=F32)
-        psend[:, g, :, 0:128] = a.reshape(nz, own, HD)
-        psend[:, g, :, 128:256] = jnp.where(lane < 64, m, total).reshape(nz, own, 128)
+        some = total > 0
+        a = a / jnp.where(some, total, 1.0)
+        psend[:, g, :, 0:128] = a.astype(BF16).reshape(nz, own, HD)
+        both = jnp.where(lane % 2 == 0, m, total)
+        big = both.astype(BF16)
+        rest = both - big.astype(F32)
+        mid = rest.astype(BF16)
+        low = (rest - mid.astype(F32)).astype(BF16)
+        triple = jnp.where(lane < 32, big.astype(F32), jnp.where(lane < 64, mid.astype(F32), low.astype(F32)))
+        psend[:, g, :, 128:256] = triple.astype(BF16).reshape(nz, own, 128)
     for d in range(1, nz):
         to = lax.rem(me + d, nz)
         begin(None, remote(psend.at[to], precv.at[me], ps.at[d - 1], pr.at[d - 1], at_z(to)))
@@ -267,16 +304,21 @@
         remote(src, src, ps.at[d - 1], pr.at[d - 1], at_z(lax.rem(me + d, nz))).wait_recv()
 
     for g in range(heads):
-        parts = [cst[g]] + [precv[p, g] for p in range(nz)]
-        top = parts[0][:, 128:129]
+        parts = [(cst[g, :, 0:128], cst[g, :, 128:129], cst[g, :, 192:193], None)]
+        for p in range(nz):
+            t = precv[p, g].astype(F32)
+            m = (t[:, 128:129] + t[:, 160:161]) + t[:, 192:193]
+            l = (t[:, 129:130] + t[:, 161:162]) + t[:, 193:194]
+            parts.append((t[:, 0:128], m, l, l))
+        top = parts[0][1]
         for t in parts[1:]:
-            top = jnp.maximum(top, t[:, 128:129])
+            top = jnp.maximum(top, t[1])
         total = jnp.zeros((own, 1), F32)
         a = jnp.zeros((own, HD), F32)
         for t in parts:
-            e = jnp.exp(t[:, 128:129] - top)
-            total = total + e * t[:, 192:193]
-            a = a + e * t[:, 0:128]
+            e = jnp.exp(t[1] - top)
+            total = total + e * t[2]
+            a = a + (e if t[3] is None else e * t[3]) * t[0]
         asend[g] = (a / total).astype(BF16)
     for d in range(1, nz):
         begin(None, remote(asend, arecv.at[me], as_.at[d - 1], ar.at[d - 1], at_z(lax.rem(me + d, nz))))
@@ -330,26 +372,30 @@
     own = reqs * steps * QPK
     oc = out_weight.shape[1]
     slots = cache_key.shape[1]
-    gain = lax.dynamic_slice(norm_gain, (lax.axis_index("head") * xc,), (xc,)).astype(F32).reshape(1, xc)
-    target = block_owner[:, 0] * reqs + block_slot
-    code = jnp.where(jnp.arange(BLK, dtype=jnp.int32)[None, :] < block_len[:, None], target[:, None], -1)
-    code = code.reshape(1, tokens)
-    q = query.reshape(reqs, steps, heads, QPK, HD).transpose(2, 0, 1, 3, 4).reshape(heads, own, HD)
-    pieces = max(1, wr // 512)
+    pieces = max(1, wr // 256)
     xpieces = 4
     ro = nz * reqs // nh
     zc = (nz - 1) * pieces
     xcnt = (nh // 2 - 1) * xpieces
     dma = pltpu.SemaphoreType.DMA
     vm = pl.BlockSpec(memory_space=pltpu.VMEM)
-    sm = pl.BlockSpec(memory_space=pltpu.SMEM)
     hb = pl.BlockSpec(memory_space=pl.ANY)
     return pl.pallas_call(
         functools.partial(kernel, nz, nh, pieces, xpieces),
         out_shape=jax.ShapeDtypeStruct((ro, steps, oc), BF16),
-        in_specs=[vm, vm, sm, vm, vm, vm, hb, hb, hb, hb, hb, hb],
+        in_specs=[hb] * 14,
         out_specs=vm,
         scratch_shapes=[
+            pltpu.VMEM(norm_gain.shape, BF16),
+            pltpu.SMEM(block_slot.shape, jnp.int32),
+            pltpu.SMEM(block_slot.shape, jnp.int32),
+            pltpu.SMEM(block_slot.shape, jnp.int32),
+            pltpu.SMEM(cache_len.shape, jnp.int32),
+            pltpu.VMEM(query.shape, BF16),
+            pltpu.VMEM(step_key.shape, BF16),
+            pltpu.VMEM(step_value.shape, BF16),
+            pltpu.VMEM((heads * own, HD), F32),
+            pltpu.VMEM((heads, own, HD), BF16),
             pltpu.VMEM((tokens, xc), BF16),
             pltpu.VMEM((nh, tokens, xc), BF16),
             pltpu.VMEM((nz, 2, wr, width), BF16),
@@ -357,8 +403,8 @@
             pltpu.VMEM((2, reqs, slots, width), BF16),
             pltpu.VMEM(out_weight.shape, BF16),
             pltpu.VMEM((nz, heads, own, HD), BF16),
-            pltpu.VMEM((nz, heads, own, 256), F32),
-            pltpu.VMEM((nz, heads, own, 256), F32),
+            pltpu.VMEM((nz, heads, own, 256), BF16),
+            pltpu.VMEM((nz, heads, own, 256), BF16),
             pltpu.VMEM((heads, own, 256), F32),
             pltpu.VMEM((heads, own, HD), BF16),
             pltpu.VMEM((nz, heads, own, HD), BF16),
@@ -366,7 +412,7 @@
             pltpu.VMEM((nh, ro * steps, oc), F32),
             pltpu.VMEM((nh, ro * steps, oc), F32),
             pltpu.VMEM((nh, 8, tokens), F32),
-            dma((6,)),
+            dma((14,)),
             dma((2, zc)), dma((2, zc)), dma((2, zc)), dma((2, zc)),
             dma((2, xcnt)), dma((2, xcnt)), dma((2, xcnt)), dma((2, xcnt)),
             dma((1,)), dma((1,)),
@@ -377,7 +423,7 @@
             collective_id=0, has_side_effects=True, vmem_limit_bytes=52 * 1024 * 1024
         ),
     )(
-        gain, code, cache_len, q, step_key, step_value,
+        norm_gain, block_owner[:, 0], block_slot, block_len, cache_len, query, step_key, step_value,
         prompt_states, key_weight, value_weight, cache_key, cache_value, out_weight,
     )
 

time: 107 us -> 105 us (0.981)
  Pallas kernels: 100 us -> 96.9 us
  local copies, waits for them, and re-layouts: 4.68 us -> 7.25 us
  other arithmetic: 2.09 us -> 0 us
    unnamed x9 -> x19, local copies, waits for them, and re-layouts: 3.84 us -> 7.25 us
    pallas_call x1, Pallas kernels: 100 us -> 96.9 us  [body(): pl.pallas_call(functools.partial(kernel, nz, nh, pieces, xpieces), out_sh...]
where the time goes in v2:
time: 105 us; the launch traced here: 104 us
  Pallas kernels  96.9 us (92%)
  local copies, waits for them, and re-layouts  7.25 us (7%)
    pallas_call x1, Pallas kernels, body(): pl.pallas_call(functools.partial(kernel, nz, nh, pieces, xpieces), out_sh...  96.9 us
    unnamed x19, local copies, waits for them, and re-layouts  7.25 us

profile of v2, /device:TPU:0, one launch (start us, length us, event | category | flops | bytes accessed | tf_op | source)
XLA Modules:
  0.0 104.1 jit_solution(10462796579489810021)
XLA Ops:
  0.0 0.0 copy-start
  0.0 1.2 %copy-done = bf16[2048,256]{1,0:T(8,128)(2,1)S(1)} copy-done((bf16[2048,256]{1,0:T(8,128)(2,1)S(1)}, bf16[2048,256]{1,0:T(8,128)(2,1)}, u32[]{:S(2)}) %copy-start) | copy-done | bytes 1048600
  1.2 0.0 copy-start.1
  1.2 0.7 copy-done.1
  1.9 0.0 copy-start.2
  1.9 0.7 copy-done.2
  2.7 0.0 copy-start.3
  2.7 0.7 copy-done.3
  3.3 0.0 copy-start.4
  3.3 0.7 copy-done.4
  4.0 0.0 copy-start.5
  4.0 0.7 copy-done.5
  4.7 0.0 copy-start.6
  4.7 0.7 copy-done.6
  5.3 0.0 copy-start.7
  5.3 0.7 copy-done.7
  6.0 0.0 copy-start.8
  6.0 0.7 copy-done.8
  6.6 96.9 %shard_map.136 = bf16[2,2,2048]{2,1,0:T(2,128)(2,1)S(1)} custom-call(bf16[8192]{0:T(1024)(128)(2,1)S(1)} %copy-done.1, s32[64]{0:T(128)S(1)} %bitcast.1, s32[64]{0:T(128)S(1)} %copy-done.6, s32[64]{0:T(128)S(1)} %copy-done.7, s32[2]{0:T(128)S(1)} %copy-done.8, bf16[2,2,2048]{2,1,0:T(2,128)(2,1)S(1)} %copy-done.2, bf16[2,2,256]{2,1,0:T(2,128)(2,1)S(1)} %copy-done.3, ...), custom_call_target="tpu_custom_call" | custom-call | tf_op jit(solution)/shard_map/pallas_call | solution.py:383
  103.5 0.6 copy.16
Async XLA Ops:
  0.0 1.2 %copy-start = (bf16[2048,256]{1,0:T(8,128)(2,1)S(1)}, bf16[2048,256]{1,0:T(8,128)(2,1)}, u32[]{:S(2)}) copy-start(bf16[2048,256]{1,0:T(8,128)(2,1)} %wk_hbm.1) | copy-start | bytes 3145732
  1.2 0.7 copy-start.1
  1.9 0.7 copy-start.2
  2.7 0.7 copy-start.3
  3.3 0.7 copy-start.4
  4.0 0.7 copy-start.5
  4.7 0.7 copy-start.6
  5.3 0.7 copy-start.7
  6.0 0.7 copy-start.8

commit v3 on v2

--- a/solution.py
+++ b/solution.py
@@ -295,15 +295,15 @@
         low = (rest - mid.astype(F32)).astype(BF16)
         triple = jnp.where(lane < 32, big.astype(F32), jnp.where(lane < 64, mid.astype(F32), low.astype(F32)))
         psend[:, g, :, 128:256] = triple.astype(BF16).reshape(nz, own, 128)
-    for d in range(1, nz):
-        to = lax.rem(me + d, nz)
-        begin(None, remote(psend.at[to], precv.at[me], ps.at[d - 1], pr.at[d - 1], at_z(to)))
-    precv[me] = psend[me]
-    for d in range(1, nz):
-        src = precv.at[lax.rem(me - d + nz, nz)]
-        remote(src, src, ps.at[d - 1], pr.at[d - 1], at_z(lax.rem(me + d, nz))).wait_recv()
+        for d in range(1, nz):
+            to = lax.rem(me + d, nz)
+            begin(None, remote(psend.at[to, g], precv.at[me, g], ps.at[d - 1, g], pr.at[d - 1, g], at_z(to)))
+        precv[me, g] = psend[me, g]
 
     for g in range(heads):
+        for d in range(1, nz):
+            src = precv.at[lax.rem(me - d + nz, nz), g]
+            remote(src, src, ps.at[d - 1, g], pr.at[d - 1, g], at_z(lax.rem(me + d, nz))).wait_recv()
         parts = [(cst[g, :, 0:128], cst[g, :, 128:129], cst[g, :, 192:193], None)]
         for p in range(nz):
             t = precv[p, g].astype(F32)
@@ -320,15 +320,16 @@
             total = total + e * t[2]
             a = a + (e if t[3] is None else e * t[3]) * t[0]
         asend[g] = (a / total).astype(BF16)
-    for d in range(1, nz):
-        begin(None, remote(asend, arecv.at[me], as_.at[d - 1], ar.at[d - 1], at_z(lax.rem(me + d, nz))))
-    arecv[me] = asend[...]
-    for d in range(1, nz):
-        src = arecv.at[lax.rem(me - d + nz, nz)]
-        remote(src, src, as_.at[d - 1], ar.at[d - 1], at_z(lax.rem(me + d, nz))).wait_recv()
+        for d in range(1, nz):
+            to = at_z(lax.rem(me + d, nz))
+            begin(None, remote(asend.at[g], arecv.at[me, g], as_.at[d - 1, g], ar.at[d - 1, g], to))
+        arecv[me, g] = asend[g]
 
     cow.wait()
     for g in range(heads):
+        for d in range(1, nz):
+            src = arecv.at[lax.rem(me - d + nz, nz), g]
+            remote(src, src, as_.at[d - 1, g], ar.at[d - 1, g], at_z(lax.rem(me + d, nz))).wait_recv()
         af[g * nz * own : (g + 1) * nz * own, :] = arecv[:, g].reshape(nz * own, HD).astype(F32)
     every = nz * reqs * steps
     pieces_in = [
@@ -379,7 +380,7 @@
     xcnt = (nh // 2 - 1) * xpieces
     dma = pltpu.SemaphoreType.DMA
     vm = pl.BlockSpec(memory_space=pltpu.VMEM)
-    hb = pl.BlockSpec(memory_space=pl.ANY)
+    hb = pl.BlockSpec(memory_space=pltpu.HBM)
     return pl.pallas_call(
         functools.partial(kernel, nz, nh, pieces, xpieces),
         out_shape=jax.ShapeDtypeStruct((ro, steps, oc), BF16),
@@ -416,7 +417,7 @@
             dma((2, zc)), dma((2, zc)), dma((2, zc)), dma((2, zc)),
             dma((2, xcnt)), dma((2, xcnt)), dma((2, xcnt)), dma((2, xcnt)),
             dma((1,)), dma((1,)),
-            dma((nz - 1,)), dma((nz - 1,)), dma((nz - 1,)), dma((nz - 1,)), dma((nz - 1,)), dma((nz - 1,)),
+            dma((nz - 1,)), dma((nz - 1,)), dma((nz - 1, heads)), dma((nz - 1, heads)), dma((nz - 1, heads)), dma((nz - 1, heads)),
             dma((nh - 1,)), dma((nh - 1,)), dma((nh - 1,)), dma((nh - 1,)),
         ],
         compiler_params=pltpu.CompilerParams(

time: 105 us -> 105 us (level)
  no operation moved by 1% of the time
where the time goes in v3:
time: 105 us; the launch traced here: 104 us
  Pallas kernels  96.9 us (92%)
  local copies, waits for them, and re-layouts  7.25 us (7%)
    pallas_call x1, Pallas kernels, body(): pl.pallas_call(functools.partial(kernel, nz, nh, pieces, xpieces), out_sh...  96.9 us
    unnamed x19, local copies, waits for them, and re-layouts  7.25 us

profile of v3, /device:TPU:0, one launch (start us, length us, event | category | flops | bytes accessed | tf_op | source)
XLA Modules:
  0.0 104.1 jit_solution(455131480216629111)
XLA Ops:
  0.0 0.0 copy-start
  0.0 1.2 %copy-done = bf16[2048,256]{1,0:T(8,128)(2,1)S(1)} copy-done((bf16[2048,256]{1,0:T(8,128)(2,1)S(1)}, bf16[2048,256]{1,0:T(8,128)(2,1)}, u32[]{:S(2)}) %copy-start) | copy-done | bytes 1048600
  1.2 0.0 copy-start.1
  1.2 0.7 copy-done.1
  1.9 0.0 copy-start.2
  1.9 0.7 copy-done.2
  2.7 0.0 copy-start.3
  2.7 0.7 copy-done.3
  3.3 0.0 copy-start.4
  3.3 0.7 copy-done.4
  4.0 0.0 copy-start.5
  4.0 0.7 copy-done.5
  4.7 0.0 copy-start.6
  4.7 0.7 copy-done.6
  5.3 0.0 copy-start.7
  5.3 0.7 copy-done.7
  6.0 0.0 copy-start.8
  6.0 0.7 copy-done.8
  6.6 96.9 %shard_map.136 = bf16[2,2,2048]{2,1,0:T(2,128)(2,1)S(1)} custom-call(bf16[8192]{0:T(1024)(128)(2,1)S(1)} %copy-done.1, s32[64]{0:T(128)S(1)} %bitcast.1, s32[64]{0:T(128)S(1)} %copy-done.6, s32[64]{0:T(128)S(1)} %copy-done.7, s32[2]{0:T(128)S(1)} %copy-done.8, bf16[2,2,2048]{2,1,0:T(2,128)(2,1)S(1)} %copy-done.2, bf16[2,2,256]{2,1,0:T(2,128)(2,1)S(1)} %copy-done.3, ...), custom_call_target="tpu_custom_call" | custom-call | tf_op jit(solution)/shard_map/pallas_call | solution.py:384
  103.5 0.6 copy.16
Async XLA Ops:
  0.0 1.2 %copy-start = (bf16[2048,256]{1,0:T(8,128)(2,1)S(1)}, bf16[2048,256]{1,0:T(8,128)(2,1)}, u32[]{:S(2)}) copy-start(bf16[2048,256]{1,0:T(8,128)(2,1)} %wk_hbm.1) | copy-start | bytes 3145732
  1.2 0.7 copy-start.1
  1.9 0.7 copy-start.2
  2.7 0.7 copy-start.3
  3.3 0.7 copy-start.4
  4.0 0.7 copy-start.5
  4.7 0.7 copy-start.6
  5.3 0.7 copy-start.7
  6.0 0.7 copy-start.8
